TPU v7x, 32 devices: a whole 2x2x4 slice. The times are simulated.
32 devices in a mesh: sta: 16 (over z, y, x), tm: 2 (over core).
Axes of the slice: x: 2, y: 2, z: 4, core: 2. Of those that a mesh axis runs over, the one named last changes fastest.
Arguments:
- strain: bfloat16 [24000, 4096], P('tm', 'sta')
- masks: int32 [2], replicated, may hold values from 1 to 15, as said below
- pair_local: int32 [2, 4096], P(None, 'sta'), may hold values from 0 to 255
- pair_remote: int32 [2, 4096], P(None, 'sta'), may hold values from 0 to 255
- owner: int32 [8192, 1], P('sta'), may hold values from 0 to 15; in each aligned block of 512 rows (0 to 511, 512 to 1023, ...) at most 64 rows name the same one
Outputs:
- correlations: float32 [16384, 512], P('sta', 'tm')
Inputs may be any that keep to these rules, and one draw needn't show every extreme that they name: `masks`: the 2 entries are distinct, and one of them is 15. At most 64 of the 512 pairs of one station group have the same owner.
All inputs are finite; a program needn't handle non-finite values.
Results may differ from a plain program's by a relative error of at most 0.0051.
Values may be sent and summed in bfloat16 or wider, within the bound.
A program may use at most 64 MiB of HBM per device.

v0:
```python
import math

import jax
import jax.numpy as jnp
import ml_dtypes
import numpy as np
from jax import lax
from jax.experimental import pallas as pl
from jax.experimental.pallas import tpu as pltpu
from jax.sharding import PartitionSpec as P

SEG_LEN = 6000
FREQS = 512
WIN = 32
LAGS = 512
EPSILON = 1e-06
BF16 = jnp.bfloat16


def angles_of(product):
    return np.mod(product, SEG_LEN).astype(np.float32) * np.float32(2.0 * math.pi / SEG_LEN)


def forward_table():
    angles = angles_of(np.arange(1, FREQS + 1)[:, None] * np.arange(SEG_LEN)[None, :])
    return np.concatenate([np.cos(angles), -np.sin(angles)], axis=0).astype(ml_dtypes.bfloat16)


def inverse_table():
    angles = angles_of(np.arange(1, FREQS + 1)[:, None] * (np.arange(LAGS) - LAGS // 2)[None, :])
    return np.concatenate([np.cos(angles), -np.sin(angles)], axis=0).astype(ml_dtypes.bfloat16)


def band_table():
    row = np.arange(FREQS)
    return (np.abs(row[:, None] - row[None, :]) <= WIN).astype(ml_dtypes.bfloat16)


def matmul(spec, left, right):
    return jnp.einsum(spec, left, right, preferred_element_type=jnp.float32)


def whiten(spectra):
    real_part = spectra[:, :FREQS]
    imag_part = spectra[:, FREQS:]
    amplitude = jnp.sqrt(real_part * real_part + imag_part * imag_part)
    high = amplitude.astype(BF16)
    low = (amplitude - high.astype(jnp.float32)).astype(BF16)
    band = jnp.asarray(band_table())
    total = matmul("kj,sjc->skc", band, high) + matmul("kj,sjc->skc", band, low)
    inverse = 1.0 / (total * (1.0 / (2 * WIN + 1)) + EPSILON)
    return (spectra * jnp.concatenate([inverse, inverse], axis=1)).astype(BF16)


def exchange_with(mask, group_count, arrays):
    pairs = [(i, i ^ mask) for i in range(group_count)]
    return tuple(lax.ppermute(a, "sta", pairs) for a in arrays)


def swap_other(other, group_count, arrays):
    def branch(mask):
        return lambda *given: exchange_with(mask, group_count, given)

    branches = [branch(mask) for mask in range(1, group_count - 1)]
    return lax.switch(other - 1, branches, *arrays)


def to_owners(outgoing, group_count, capacity):
    width = outgoing.shape[1]

    def kernel(out_ref, in_ref, own_sem, send_sems, recv_sems):
        me = lax.axis_index("sta")
        barrier = pltpu.get_barrier_semaphore()
        for step in range(1, group_count):
            pl.semaphore_signal(
                barrier,
                inc=1,
                device_id={"sta": (me + step) % group_count},
                device_id_type=pl.DeviceIdType.MESH,
            )
        mine = pl.ds(pl.multiple_of(me * capacity, capacity), capacity)
        own = pltpu.make_async_copy(out_ref.at[mine], in_ref.at[mine], own_sem)
        own.start()
        pl.semaphore_wait(barrier, group_count - 1)
        copies = []
        for step in range(1, group_count):
            target = (me + step) % group_count
            rows = pl.ds(pl.multiple_of(target * capacity, capacity), capacity)
            copy = pltpu.make_async_remote_copy(
                src_ref=out_ref.at[rows],
                dst_ref=in_ref.at[mine],
                send_sem=send_sems.at[step - 1],
                recv_sem=recv_sems.at[step - 1],
                device_id={"sta": target},
                device_id_type=pl.DeviceIdType.MESH,
            )
            copy.start()
            copies.append(copy)
        own.wait()
        for copy in copies:
            copy.wait()

    return pl.pallas_call(
        kernel,
        out_shape=jax.ShapeDtypeStruct((group_count * capacity, width), BF16),
        in_specs=[pl.BlockSpec(memory_space=pltpu.VMEM)],
        out_specs=pl.BlockSpec(memory_space=pltpu.VMEM),
        scratch_shapes=[
            pltpu.SemaphoreType.DMA(()),
            pltpu.SemaphoreType.DMA((group_count - 1,)),
            pltpu.SemaphoreType.DMA((group_count - 1,)),
        ],
        compiler_params=pltpu.CompilerParams(collective_id=0, has_side_effects=True),
    )(outgoing)


def one_hot(index, count):
    return (index[None, :] == jnp.arange(count, dtype=jnp.int32)[:, None]).astype(BF16)


def cross_of(kept, arrived, kept_index, arrived_index, sign):
    channels = kept.shape[1]
    mine = matmul("kc,cp->kp", kept, one_hot(kept_index, channels))
    theirs = matmul("kc,cp->kp", arrived, one_hot(arrived_index, channels))
    ar, ai, br, bi = mine[:FREQS], mine[FREQS:], theirs[:FREQS], theirs[FREQS:]
    return jnp.concatenate([ar * br + ai * bi, (ai * br - ar * bi) * sign], axis=0).astype(BF16)


def targets_of(owners, group_count, capacity):
    hot = (owners[:, None] == jnp.arange(group_count, dtype=jnp.int32)[None, :]).astype(jnp.float32)
    rows = np.arange(owners.shape[0])
    before = (rows[None, :] < rows[:, None]).astype(ml_dtypes.bfloat16)
    earlier = matmul("ij,jo->io", jnp.asarray(before), hot.astype(BF16))
    return owners * capacity + jnp.sum(earlier * hot, axis=1).astype(jnp.int32)


def per_device(strain, masks, pair_local, pair_remote, owner):
    group_count = lax.axis_size("sta")
    time_count = lax.axis_size("tm")
    seg_count = strain.shape[0] // SEG_LEN
    channels = strain.shape[1]
    round_count, pair_count = pair_local.shape
    capacity = max(2, 2 * round_count * pair_count // group_count)
    full_mask = group_count - 1
    other = masks[0] + masks[1] - full_mask
    full_first = masks[0] == full_mask

    def by_mask(array):
        return jnp.where(full_first, array[0], array[1]), jnp.where(full_first, array[1], array[0])

    targets = targets_of(owner[:, 0], group_count, capacity)
    targets = jnp.concatenate(by_mask(targets.reshape(round_count, pair_count)))
    local_index, remote_index = by_mask(pair_local), by_mask(pair_remote)
    index = [jnp.stack(pair) for pair in zip(local_index, remote_index)]

    upper = jnp.bitwise_and(lax.axis_index("sta"), jnp.bitwise_and(other, -other)) != 0
    upper = upper.astype(jnp.int32)
    segments = strain.reshape(seg_count, SEG_LEN, channels)
    table = jnp.asarray(forward_table())

    def whitened_of(number):
        segment = lax.dynamic_slice_in_dim(segments, number, 1, axis=0)
        return whiten(matmul("kl,slc->skc", table, segment))[0]

    sent = whitened_of(upper)
    full_peer = exchange_with(group_count - 1, group_count, (index[0], sent))
    other_peer = swap_other(other, group_count, (sent, index[1]))
    kept_number, other_sent, other_index = lax.optimization_barrier((1 - upper, *other_peer))
    kept = whitened_of(kept_number)

    sign = np.concatenate([np.ones(pair_count), -np.ones(pair_count)]).astype(np.float32)[None, :]
    inverse = jnp.asarray(inverse_table())
    norm_scale = 1.0 / math.sqrt(seg_count * time_count * FREQS)
    width = LAGS // time_count
    first_half = lax.axis_index("tm") == 0

    def lags_of(number, peer, peer_index):
        kept_index = jnp.concatenate([local_index[number], peer_index[1]])
        arrived_index = jnp.concatenate([remote_index[number], peer_index[0]])
        cross = cross_of(kept, peer, kept_index, arrived_index, sign)
        lagged = matmul("kp,kl->pl", cross, inverse) * norm_scale
        halves = lagged[:, :width], lagged[:, width:]
        mine = jnp.where(first_half, halves[0], halves[1])
        theirs = jnp.where(first_half, halves[1], halves[0]).astype(BF16)
        return mine + lax.ppermute(theirs, "tm", [(0, 1), (1, 0)]).astype(jnp.float32)

    other_lags = lags_of(1, other_sent, other_index)
    full_lags = lags_of(0, full_peer[1], full_peer[0])
    [full_back] = exchange_with(group_count - 1, group_count, (full_lags[pair_count:].astype(BF16),))
    [other_back] = swap_other(other, group_count, (other_lags[pair_count:].astype(BF16),))
    full_total = full_lags[:pair_count] + full_back.astype(jnp.float32)
    other_total = other_lags[:pair_count] + other_back.astype(jnp.float32)
    rows = jnp.concatenate([full_total, other_total]).astype(BF16)
    outgoing = matmul("ps,pl->sl", one_hot(targets, group_count * capacity).T, rows).astype(BF16)
    return to_owners(outgoing, group_count, capacity).astype(jnp.float32)


def solution(mesh):
    placed = (P("tm", "sta"), P(), P(None, "sta"), P(None, "sta"), P("sta", None))
    return jax.shard_map(
        per_device, mesh=mesh, in_specs=placed, out_specs=P("sta", "tm"), check_vma=False
    )
```

profile of v0, /device:TPU:12, one launch (start us, length us, event | category | flops | bytes accessed | tf_op | source)
XLA Modules:
  0.0 110.0 jit_solution(1003901117761936418)
XLA Ops:
  0.0 1.3 %fusion.67 = (s32[1]{0:T(128)}, s32[1]{0:T(128)}) fusion(s32[2]{0:T(128)} %param.40), kind=kLoop, calls=%fused_computation.107 | loop fusion | bytes 16 | tf_op jit(solution)/shard_map/slice | solution.py:145
  2.5 7.4 %fusion.4 = f32[1,1024,256]{1,2,0:T(8,128)S(1)} fusion(bf16[1024,6000]{1,0:T(8,128)(2,1)} %constant.53.clone, bf16[2,6000,256]{2,1,0:T(8,128)(2,1)} %bitcast.80, s32[]{:T(128)S(6)} %select_n.76), kind=kOutput, calls=%fused_computation.7 | convolution fusion | flops 3145728000 | bytes 16441348 | tf_op jit(solution)/shard_map/kl,slc->skc/dot_general | solution.py:40
  10.8 0.9 fusion.21
  11.7 2.4 %collective-permute-start.43 = (bf16[1024,256]{0,1:T(8,128)(2,1)}, bf16[1024,256]{0,1:T(8,128)(2,1)S(1)}, u32[]{:S(2)}, u32[]{:S(2)}) collective-permute-start(bf16[1024,256]{0,1:T(8,128)(2,1)} %fusion.21), channel_id=1, source_target_pairs={{0,30},{2,28},{4,26},{6,24},{8,22},{10,20},{12,18},{14,16},{16,14}... | collective-permute-start | bytes 1572872 | tf_op jit(solution)/shard_map/ppermute | solution.py:57
  14.8 34.7 %conditional.5 = (bf16[1024,256]{1,0:T(8,128)(2,1)}, s32[2,256]{1,0:T(2,128)}) conditional(s32[]{:T(128)} %bitcast.4, (bf16[1024,256]{0,1:T(8,128)(2,1)}, s32[2,256]{1,0:T(2,128)S(1)}) %tuple.162, (bf16[1024,256]{0,1:T(8,128)(2,1)}, s32[2,256]{1,0:T(2,128)S(1)}) %tuple.162, (bf16[1024,256]{0,1:T(8,128)(2,1)}, ...), branch_computations={%region_1.2_spmd, %region_2.3_spmd, %region_3.4_spmd, %region_4.5_... | conditional | bytes 3154016 | solution.py:65
  14.8 1.2 %copy.18 = bf16[1024,256]{1,0:T(8,128)(2,1)S(1)} copy(bf16[1024,256]{0,1:T(8,128)(2,1)} %get-tuple-element.146) | data formatting | bytes 1048576 | tf_op jit(solution)/shard_map
  16.1 3.5 %collective-permute-start.12 = (bf16[1024,256]{1,0:T(8,128)(2,1)S(1)}, bf16[1024,256]{1,0:T(8,128)(2,1)}, u32[]{:S(2)}, u32[]{:S(2)}) collective-permute-start(bf16[1024,256]{1,0:T(8,128)(2,1)S(1)} %copy.18), channel_id=1, source_target_pairs={{0,14},{2,12},{4,10},{6,8},{8,6},{10,4},{12,2},{14,0},{16,30},{18,... | collective-permute-start | bytes 1572872 | tf_op jit(solution)/shard_map/cond/branch_6_fun/ppermute | solution.py:57
  20.0 29.6 %collective-permute-done.13 = s32[2,256]{1,0:T(2,128)} collective-permute-done((s32[2,256]{1,0:T(2,128)S(1)}, s32[2,256]{1,0:T(2,128)}, u32[]{:S(2)}, u32[]{:S(2)}) %collective-permute-start.13) | collective-permute-done | bytes 2080 | tf_op jit(solution)/shard_map/cond/branch_6_fun/ppermute | solution.py:57
  49.5 0.7 fusion.66
  50.3 7.4 %fusion.3 = f32[1,1024,256]{1,2,0:T(8,128)S(1)} fusion(bf16[1024,6000]{1,0:T(8,128)(2,1)} %constant.53.clone, bf16[2,6000,256]{2,1,0:T(8,128)(2,1)} %bitcast.81, s32[]{:T(128)S(6)} %select_n.80), kind=kOutput, calls=%fused_computation.6 | convolution fusion | flops 3145728000 | bytes 16441348 | tf_op jit(solution)/shard_map/kl,slc->skc/dot_general | solution.py:40
  58.5 1.5 %fusion.33 = f32[1024,512]{1,0:T(8,128)S(1)} fusion(bf16[1024,256]{1,0:T(8,128)(2,1)} %get-tuple-element.133, s32[512]{0:T(512)S(1)} %pad_add_fusion.6), kind=kOutput, calls=%fused_computation.61 | convolution fusion | flops 268566528 | bytes 2623488 | tf_op jit(solution)/shard_map/kc,cp->kp/dot_general | solution.py:40
  62.1 0.7 fusion.5
  63.0 0.8 collective-permute-start.42
  64.1 4.3 %collective-permute-done.42 = s32[2,256]{1,0:T(2,128)S(1)} collective-permute-done((s32[2,256]{1,0:T(2,128)S(1)}, s32[2,256]{1,0:T(2,128)S(1)}, u32[]{:S(2)}, u32[]{:S(2)}) %collective-permute-start.42) | collective-permute-done | bytes 2080 | tf_op jit(solution)/shard_map/ppermute | solution.py:57
  70.2 0.7 fusion.6
  71.2 7.9 %conditional.6 = (bf16[256,256]{1,0:T(8,128)(2,1)}) conditional(s32[]{:T(128)} %bitcast.4, bf16[256,256]{1,0:T(8,128)(2,1)S(1)} %slice.279, bf16[256,256]{1,0:T(8,128)(2,1)S(1)} %slice.279, bf16[256,256]{1,0:T(8,128)(2,1)S(1)} %slice.279, bf16[256,256]{1,0:T(8,128)(2,1)S(1)} %slice.279, ...), branch_computations={%region_15.16_spmd, %region_16.17_spmd, %region_17.18_spmd, %regio... | conditional | bytes 524336
  71.3 1.3 %collective-permute-start.34 = (bf16[256,256]{1,0:T(8,128)(2,1)S(1)}, bf16[256,256]{1,0:T(8,128)(2,1)}, u32[]{:S(2)}, u32[]{:S(2)}) collective-permute-start(bf16[256,256]{1,0:T(8,128)(2,1)S(1)} %param.20), channel_id=1, source_target_pairs={{0,14},{2,12},{4,10},{6,8},{8,6},{10,4},{12,2},{14,0},{16,30},{18,... | collective-permute-start | bytes 393224 | tf_op jit(solution)/shard_map/cond/branch_6_fun/ppermute | solution.py:57
  72.5 6.6 %collective-permute-done.34 = bf16[256,256]{1,0:T(8,128)(2,1)} collective-permute-done((bf16[256,256]{1,0:T(8,128)(2,1)S(1)}, bf16[256,256]{1,0:T(8,128)(2,1)}, u32[]{:S(2)}, u32[]{:S(2)}) %collective-permute-start.34) | collective-permute-done | bytes 131104 | tf_op jit(solution)/shard_map/cond/branch_6_fun/ppermute | solution.py:57
  79.3 0.8 collective-permute-start.45
  80.1 0.9 fusion.38
  81.0 8.0 %collective-permute-done.45 = bf16[256,256]{1,0:T(8,128)(2,1)S(1)} collective-permute-done((bf16[256,256]{1,0:T(8,128)(2,1)S(1)}, bf16[256,256]{1,0:T(8,128)(2,1)S(1)}, u32[]{:S(2)}, u32[]{:S(2)}) %collective-permute-start.45) | collective-permute-done | bytes 131104 | tf_op jit(solution)/shard_map/ppermute | solution.py:57
  89.1 1.3 %fusion.7.out_ref = bf16[1024,256]{1,0:T(8,128)(2,1)} fusion(s32[512]{0:T(512)S(1)} %pad_add_fusion, bf16[256,256]{1,0:T(8,128)(2,1)S(1)} %fusion.38, bf16[256,256]{1,0:T(8,128)(2,1)S(1)} %fusion.39), kind=kOutput, calls=%fused_computation.12 | convolution fusion | flops 269746176 | bytes 788480 | tf_op jit(solution)/shard_map/ps,pl->sl/dot_general | solution.py:40
  90.4 17.6 %shard_map.109 = bf16[1024,256]{1,0:T(8,128)(2,1)} custom-call(bf16[1024,256]{1,0:T(8,128)(2,1)} %fusion.7.out_ref), custom_call_target="tpu_custom_call" | custom-call | tf_op jit(solution)/shard_map/pallas_call | solution.py:103
  107.9 2.1 %convert_element_type.147 = f32[1024,256]{1,0:T(8,128)} convert(bf16[1024,256]{1,0:T(8,128)(2,1)} %shard_map.109) | non-fusion elementwise | flops 262144 | bytes 1572864 | tf_op jit(solution)/shard_map/convert_element_type | solution.py:195
  (51 shorter events, 6.6 us)
Async XLA Ops:
  2.5 7.5 %copy-start.2 = (bf16[512,512]{1,0:T(8,128)(2,1)S(1)}, bf16[512,512]{1,0:T(8,128)(2,1)}, u32[]{:S(2)}) copy-start(bf16[512,512]{1,0:T(8,128)(2,1)} %constant.54.clone) | copy-start | bytes 1572868
  10.4 4.4 %copy-start.6 = (s32[2,256]{1,0:T(2,128)S(1)}, s32[2,256]{1,0:T(2,128)}, u32[]{:S(2)}) copy-start(s32[2,256]{1,0:T(2,128)} %param.42) | copy-start | bytes 6148
  10.4 4.4 %copy-start.7 = (s32[2,256]{1,0:T(2,128)S(1)}, s32[2,256]{1,0:T(2,128)}, u32[]{:S(2)}) copy-start(s32[2,256]{1,0:T(2,128)} %param.41) | copy-start | bytes 6148
  11.7 57.3 %collective-permute-start.43 = (bf16[1024,256]{0,1:T(8,128)(2,1)}, bf16[1024,256]{0,1:T(8,128)(2,1)S(1)}, u32[]{:S(2)}, u32[]{:S(2)}) collective-permute-start(bf16[1024,256]{0,1:T(8,128)(2,1)} %fusion.21), channel_id=1, source_target_pairs={{0,30},{2,28},{4,26},{6,24},{8,22},{10,20},{12,18},{14,16},{16,14}... | collective-permute-start | bytes 1572872 | tf_op jit(solution)/shard_map/ppermute | solution.py:57
  16.1 33.4 %collective-permute-start.12 = (bf16[1024,256]{1,0:T(8,128)(2,1)S(1)}, bf16[1024,256]{1,0:T(8,128)(2,1)}, u32[]{:S(2)}, u32[]{:S(2)}) collective-permute-start(bf16[1024,256]{1,0:T(8,128)(2,1)S(1)} %copy.18), channel_id=1, source_target_pairs={{0,14},{2,12},{4,10},{6,8},{8,6},{10,4},{12,2},{14,0},{16,30},{18,... | collective-permute-start | bytes 1572872 | tf_op jit(solution)/shard_map/cond/branch_6_fun/ppermute | solution.py:57
  19.6 30.0 %collective-permute-start.13 = (s32[2,256]{1,0:T(2,128)S(1)}, s32[2,256]{1,0:T(2,128)}, u32[]{:S(2)}, u32[]{:S(2)}) collective-permute-start(s32[2,256]{1,0:T(2,128)S(1)} %get-tuple-element.109), channel_id=1, source_target_pairs={{0,14},{2,12},{4,10},{6,8},{8,6},{10,4},{12,2},{14,0},{16,30},{18,... | collective-permute-start | bytes 6152 | tf_op jit(solution)/shard_map/cond/branch_6_fun/ppermute | solution.py:57
  60.0 1.0 copy-start.1
  61.0 1.0 copy-start
  61.0 1.0 copy-start.4
  62.1 1.7 %copy-start.3 = (bf16[512,512]{1,0:T(8,128)(2,1)S(1)}, bf16[512,512]{1,0:T(8,128)(2,1)}, u32[]{:S(2)}) copy-start(bf16[512,512]{1,0:T(8,128)(2,1)} %constant.52.clone) | copy-start | bytes 1572868
  62.1 1.7 %copy-start.5 = (s32[512,1]{0,1:T(1,128)S(1)}, s32[512,1]{0,1:T(1,128)}, u32[]{:S(2)}) copy-start(s32[512,1]{0,1:T(1,128)} %param.43) | copy-start | bytes 6148
  62.9 8.2 %collective-permute-start.46 = (bf16[512,256]{1,0:T(8,128)(2,1)S(1)}, bf16[512,256]{1,0:T(8,128)(2,1)S(1)}, u32[]{:S(2)}, u32[]{:S(2)}) collective-permute-start(bf16[512,256]{1,0:T(8,128)(2,1)S(1)} %select_convert_fusion), channel_id=1, source_target_pairs={{0,1},{1,0},{2,3},{3,2},{4,5},{5,4},{6,7},{7,6},{8,9},{9,8},{10,11... | collective-permute-start | bytes 786440 | tf_op jit(solution)/shard_map/ppermute | solution.py:185
  63.0 5.4 %collective-permute-start.42 = (s32[2,256]{1,0:T(2,128)S(1)}, s32[2,256]{1,0:T(2,128)S(1)}, u32[]{:S(2)}, u32[]{:S(2)}) collective-permute-start(s32[2,256]{1,0:T(2,128)S(1)} %pad_add_fusion.2), channel_id=1, source_target_pairs={{0,30},{2,28},{4,26},{6,24},{8,22},{10,20},{12,18},{14,16},{16,14}... | collective-permute-start | bytes 6152 | tf_op jit(solution)/shard_map/ppermute | solution.py:57
  71.0 8.1 %collective-permute-start.44 = (bf16[512,256]{1,0:T(8,128)(2,1)S(1)}, bf16[512,256]{1,0:T(8,128)(2,1)S(1)}, u32[]{:S(2)}, u32[]{:S(2)}) collective-permute-start(bf16[512,256]{1,0:T(8,128)(2,1)S(1)} %select_convert_fusion.1), channel_id=1, source_target_pairs={{0,1},{1,0},{2,3},{3,2},{4,5},{5,4},{6,7},{7,6},{8,9},{9,8},{10,11... | collective-permute-start | bytes 786440 | tf_op jit(solution)/shard_map/ppermute | solution.py:185
  71.3 7.9 %collective-permute-start.34 = (bf16[256,256]{1,0:T(8,128)(2,1)S(1)}, bf16[256,256]{1,0:T(8,128)(2,1)}, u32[]{:S(2)}, u32[]{:S(2)}) collective-permute-start(bf16[256,256]{1,0:T(8,128)(2,1)S(1)} %param.20), channel_id=1, source_target_pairs={{0,14},{2,12},{4,10},{6,8},{8,6},{10,4},{12,2},{14,0},{16,30},{18,... | collective-permute-start | bytes 393224 | tf_op jit(solution)/shard_map/cond/branch_6_fun/ppermute | solution.py:57
  79.3 9.8 %collective-permute-start.45 = (bf16[256,256]{1,0:T(8,128)(2,1)S(1)}, bf16[256,256]{1,0:T(8,128)(2,1)S(1)}, u32[]{:S(2)}, u32[]{:S(2)}) collective-permute-start(bf16[256,256]{1,0:T(8,128)(2,1)S(1)} %slice.280), channel_id=1, source_target_pairs={{0,30},{2,28},{4,26},{6,24},{8,22},{10,20},{12,18},{14,16},{16,14}... | collective-permute-start | bytes 393224 | tf_op jit(solution)/shard_map/ppermute | solution.py:57
where the time goes:
time: 110 us
  waiting for transfers between devices  48.5 us (44%)
  matrix products  23.9 us (22%)
  Pallas kernels  17.6 us (16%)
  starting transfers between devices  9.34 us (8%)
  other arithmetic  4.34 us (4%)
  local copies, waits for them, and re-layouts  4.18 us (4%)
  between operations  2.09 us (2%)
    ppermute x6, waiting for transfers between devices, exchange_with(): return tuple((lax.ppermute(a, 'sta', pairs) for a in arrays))  48.5 us
    dot_general x16, matrix products, matmul(): return jnp.einsum(spec, left, right, preferred_element_type=jnp.float32)  23.9 us
    pallas_call x1, Pallas kernels, to_owners(): pl.pallas_call(kernel, out_shape=jax.ShapeDtypeStruct((group_count * capa...  17.6 us
    ppermute x6, starting transfers between devices, exchange_with(): return tuple((lax.ppermute(a, 'sta', pairs) for a in arrays))  9.19 us
  transfers between devices with their start and end apart: 8, of which 4 were waited for; matrix products, arithmetic and copies ran while one was open for 16% of the time, Pallas kernels for 0%

commit v1 on v0

--- a/solution.py
+++ b/solution.py
@@ -57,11 +57,10 @@
     return tuple(lax.ppermute(a, "sta", pairs) for a in arrays)
 
 
-def swap_other(other, group_count, arrays):
-    def branch(mask):
-        return lambda *given: exchange_with(mask, group_count, given)
-
-    branches = [branch(mask) for mask in range(1, group_count - 1)]
+def switched(other, group_count, run, *arrays):
+    branches = [
+        lambda *given, mask=mask: run(mask, *given) for mask in range(1, group_count - 1)
+    ]
     return lax.switch(other - 1, branches, *arrays)
 
 
@@ -162,11 +161,15 @@
         segment = lax.dynamic_slice_in_dim(segments, number, 1, axis=0)
         return whiten(matmul("kl,slc->skc", table, segment))[0]
 
-    sent = whitened_of(upper)
-    full_peer = exchange_with(group_count - 1, group_count, (index[0], sent))
-    other_peer = swap_other(other, group_count, (sent, index[1]))
-    kept_number, other_sent, other_index = lax.optimization_barrier((1 - upper, *other_peer))
-    kept = whitened_of(kept_number)
+    index_rows = jnp.concatenate(index, axis=0).astype(BF16)
+    index_rows = jnp.pad(index_rows, ((0, 16 - 2 * round_count), (0, 0)))
+    sent = jnp.concatenate([whitened_of(upper), index_rows], axis=0)
+    [full_peer] = exchange_with(group_count - 1, group_count, (sent,))
+    kept = whitened_of(1 - upper)
+    sent, kept = lax.optimization_barrier((sent, kept))
+    [other_peer] = switched(
+        other, group_count, lambda mask, a: exchange_with(mask, group_count, (a,)), sent
+    )
 
     sign = np.concatenate([np.ones(pair_count), -np.ones(pair_count)]).astype(np.float32)[None, :]
     inverse = jnp.asarray(inverse_table())
@@ -174,7 +177,10 @@
     width = LAGS // time_count
     first_half = lax.axis_index("tm") == 0
 
-    def lags_of(number, peer, peer_index):
+    def lags_of(number, arrived):
+        peer = arrived[: 2 * FREQS]
+        first = 2 * FREQS + 2 * number
+        peer_index = arrived[first : first + 2].astype(jnp.int32)
         kept_index = jnp.concatenate([local_index[number], peer_index[1]])
         arrived_index = jnp.concatenate([remote_index[number], peer_index[0]])
         cross = cross_of(kept, peer, kept_index, arrived_index, sign)
@@ -184,10 +190,18 @@
         theirs = jnp.where(first_half, halves[1], halves[0]).astype(BF16)
         return mine + lax.ppermute(theirs, "tm", [(0, 1), (1, 0)]).astype(jnp.float32)
 
-    other_lags = lags_of(1, other_sent, other_index)
-    full_lags = lags_of(0, full_peer[1], full_peer[0])
-    [full_back] = exchange_with(group_count - 1, group_count, (full_lags[pair_count:].astype(BF16),))
-    [other_back] = swap_other(other, group_count, (other_lags[pair_count:].astype(BF16),))
+    other_lags = lags_of(1, other_peer)
+    full_lags = lags_of(0, full_peer)
+    full_back, other_back = switched(
+        other,
+        group_count,
+        lambda mask, a, b: (
+            *exchange_with(group_count - 1, group_count, (a,)),
+            *exchange_with(mask, group_count, (b,)),
+        ),
+        full_lags[pair_count:].astype(BF16),
+        other_lags[pair_count:].astype(BF16),
+    )
     full_total = full_lags[:pair_count] + full_back.astype(jnp.float32)
     other_total = other_lags[:pair_count] + other_back.astype(jnp.float32)
     rows = jnp.concatenate([full_total, other_total]).astype(BF16)

time: 110 us -> 110 us (level); the launches traced: 110 us -> 109 us
  starting transfers between devices: 9.34 us -> 6.62 us
  waiting for transfers between devices: 48.5 us -> 50.7 us
  local copies, waits for them, and re-layouts: 4.18 us -> 2.38 us
    ppermute x6 -> x4, starting transfers between devices: 9.19 us -> 6.12 us  [exchange_with(): return tuple((lax.ppermute(a, 'sta', pairs) for a in arrays))]
    another operation x1 -> x0, local copies, waits for them, and re-layouts: 1.25 us -> none
    ppermute x6 -> x4, waiting for transfers between devices: 48.5 us -> 49.7 us  [exchange_with(): return tuple((lax.ppermute(a, 'sta', pairs) for a in arrays))]
    another operation x4 -> x5, other arithmetic: 0.99 us -> 2.09 us
  transfers between devices with their start and end apart: 8 -> 6, of which waited for: 4 -> 4; matrix products, arithmetic and copies ran while one was open for 16% -> 15% of each run, Pallas kernels for 0% -> 0%
where the time goes in v1:
time: 110 us; the launch traced here: 109 us
  waiting for transfers between devices  50.7 us (46%)
  matrix products  24 us (22%)
  Pallas kernels  17.5 us (16%)
  starting transfers between devices  6.62 us (6%)
  other arithmetic  5.39 us (5%)
  local copies, waits for them, and re-layouts  2.38 us (2%)
  between operations  2.09 us (2%)
    ppermute x4, waiting for transfers between devices, exchange_with(): return tuple((lax.ppermute(a, 'sta', pairs) for a in arrays))  49.7 us
    dot_general x16, matrix products, matmul(): return jnp.einsum(spec, left, right, preferred_element_type=jnp.float32)  24 us
    pallas_call x1, Pallas kernels, to_owners(): pl.pallas_call(kernel, out_shape=jax.ShapeDtypeStruct((group_count * capa...  17.5 us
    ppermute x4, starting transfers between devices, exchange_with(): return tuple((lax.ppermute(a, 'sta', pairs) for a in arrays))  6.12 us
  transfers between devices with their start and end apart: 6, of which 4 were waited for; matrix products, arithmetic and copies ran while one was open for 15% of the time, Pallas kernels for 0%

profile of v1, /device:TPU:12, one launch (start us, length us, event | category | flops | bytes accessed | tf_op | source)
XLA Modules:
  0.0 108.8 jit_solution(8220267572075087507)
XLA Ops:
  0.0 1.3 %fusion.75 = (s32[1]{0:T(128)}, s32[1]{0:T(128)}) fusion(s32[2]{0:T(128)} %param.40), kind=kLoop, calls=%fused_computation.117 | loop fusion | bytes 16 | tf_op jit(solution)/shard_map/slice | solution.py:144
  2.5 7.4 %fusion.4 = f32[1,1024,256]{1,2,0:T(8,128)S(1)} fusion(bf16[1024,6000]{1,0:T(8,128)(2,1)} %constant.57.clone, bf16[2,6000,256]{2,1,0:T(8,128)(2,1)} %bitcast.78, s32[]{:T(128)S(6)} %select_n.76), kind=kOutput, calls=%fused_computation.7 | convolution fusion | flops 3145728000 | bytes 16441348 | tf_op jit(solution)/shard_map/kl,slc->skc/dot_general | solution.py:40
  12.0 2.5 %collective-permute-start.42 = (bf16[1040,256]{1,0:T(8,128)(2,1)S(1)}, bf16[1040,256]{1,0:T(8,128)(2,1)S(1)}, u32[]{:S(2)}, u32[]{:S(2)}) collective-permute-start(bf16[1040,256]{1,0:T(8,128)(2,1)S(1)} %copy.49), channel_id=1, source_target_pairs={{0,30},{2,28},{4,26},{6,24},{8,22},{10,20},{12,18},{14,16},{16,14}... | collective-permute-start | bytes 1597448 | tf_op jit(solution)/shard_map/ppermute | solution.py:57
  14.5 7.4 %fusion.3 = f32[1,1024,256]{1,2,0:T(8,128)S(1)} fusion(bf16[1024,6000]{1,0:T(8,128)(2,1)} %constant.57.clone, bf16[2,6000,256]{2,1,0:T(8,128)(2,1)} %bitcast.79, s32[]{:T(128)S(6)} %select_n.82), kind=kOutput, calls=%fused_computation.6 | convolution fusion | flops 3145728000 | bytes 16441348 | tf_op jit(solution)/shard_map/kl,slc->skc/dot_general | solution.py:40
  22.9 43.9 %conditional.4 = (bf16[1040,256]{1,0:T(8,128)(2,1)}) conditional(s32[]{:T(128)} %bitcast.26, bf16[1040,256]{0,1:T(8,128)(2,1)S(1)} %fusion.21, bf16[1040,256]{0,1:T(8,128)(2,1)S(1)} %fusion.21, bf16[1040,256]{0,1:T(8,128)(2,1)S(1)} %fusion.21, bf16[1040,256]{0,1:T(8,128)(2,1)S(1)} %fusion.21, ...), branch_computations={%region_1.2_spmd, %region_2.3_spmd, %region_3.4_spmd, %region_4.5_... | conditional | bytes 3194928 | solution.py:64
  23.6 43.1 %collective-permute-done.11 = bf16[1040,256]{1,0:T(8,128)(2,1)} collective-permute-done((bf16[1040,256]{1,0:T(8,128)(2,1)S(1)}, bf16[1040,256]{1,0:T(8,128)(2,1)}, u32[]{:S(2)}, u32[]{:S(2)}) %collective-permute-start.11) | collective-permute-done | bytes 532512 | tf_op jit(solution)/shard_map/cond/branch_11_fun/ppermute | solution.py:57
  66.7 0.7 slice_convert_fusion
  67.4 1.6 %fusion.24 = f32[1024,512]{1,0:T(8,128)S(1)} fusion(bf16[1040,256]{1,0:T(8,128)(2,1)} %get-tuple-element.228, s32[512]{0:T(512)S(1)} %pad_add_fusion.4), kind=kOutput, calls=%fused_computation.39 | convolution fusion | flops 268566528 | bytes 2623488 | tf_op jit(solution)/shard_map/kc,cp->kp/dot_general | solution.py:40
  69.0 0.5 fusion.37
  69.6 0.7 fusion.35
  70.6 0.8 fusion.5
  73.0 0.7 fusion.34
  73.8 0.8 fusion.6
  75.1 1.1 collective-permute-done.43
  76.3 9.7 %conditional.6 = (bf16[256,256]{1,0:T(8,128)(2,1)}, bf16[256,256]{1,0:T(8,128)(2,1)}) conditional(s32[]{:T(128)} %bitcast.26, (bf16[512,256]{1,0:T(8,128)(2,1)S(1)}, bf16[512,256]{1,0:T(8,128)(2,1)S(1)}) %tuple.191, (bf16[512,256]{1,0:T(8,128)(2,1)S(1)}, bf16[512,256]{1,0:T(8,128)(2,1)S(1)}) %tuple.191, ...), branch_computations={%region_15.16_spmd, %region_16.17_spmd, %region_17.18_spmd, %regio... | conditional | bytes 1572960
  76.4 2.6 %collective-permute-start.36 = (bf16[256,256]{1,0:T(8,128)(2,1)S(1)}, bf16[256,256]{1,0:T(8,128)(2,1)}, u32[]{:S(2)}, u32[]{:S(2)}) collective-permute-start(bf16[256,256]{1,0:T(8,128)(2,1)S(1)} %slice.166), channel_id=1, source_target_pairs={{0,30},{2,28},{4,26},{6,24},{8,22},{10,20},{12,18},{14,16},{16,14}... | collective-permute-start | bytes 393224 | tf_op jit(solution)/shard_map/cond/branch_11_fun/ppermute | solution.py:57
  79.0 0.5 collective-permute-start.37
  79.5 5.2 %collective-permute-done.36 = bf16[256,256]{1,0:T(8,128)(2,1)} collective-permute-done((bf16[256,256]{1,0:T(8,128)(2,1)S(1)}, bf16[256,256]{1,0:T(8,128)(2,1)}, u32[]{:S(2)}, u32[]{:S(2)}) %collective-permute-start.36) | collective-permute-done | bytes 131104 | tf_op jit(solution)/shard_map/cond/branch_11_fun/ppermute | solution.py:57
  84.7 1.4 %collective-permute-done.37 = bf16[256,256]{1,0:T(8,128)(2,1)} collective-permute-done((bf16[256,256]{1,0:T(8,128)(2,1)S(1)}, bf16[256,256]{1,0:T(8,128)(2,1)}, u32[]{:S(2)}, u32[]{:S(2)}) %collective-permute-start.37) | collective-permute-done | bytes 131104 | tf_op jit(solution)/shard_map/cond/branch_11_fun/ppermute | solution.py:57
  86.1 0.9 fusion.43
  87.0 0.9 fusion.42
  87.9 1.3 %fusion.7.out_ref = bf16[1024,256]{1,0:T(8,128)(2,1)} fusion(s32[512]{0:T(512)S(1)} %pad_add_fusion, bf16[256,256]{1,0:T(8,128)(2,1)S(1)} %fusion.42, bf16[256,256]{1,0:T(8,128)(2,1)S(1)} %fusion.43), kind=kOutput, calls=%fused_computation.12 | convolution fusion | flops 269746176 | bytes 788480 | tf_op jit(solution)/shard_map/ps,pl->sl/dot_general | solution.py:40
  89.2 17.5 %shard_map.109 = bf16[1024,256]{1,0:T(8,128)(2,1)} custom-call(bf16[1024,256]{1,0:T(8,128)(2,1)} %fusion.7.out_ref), custom_call_target="tpu_custom_call" | custom-call | tf_op jit(solution)/shard_map/pallas_call | solution.py:102
  106.7 2.1 %convert_element_type.160 = f32[1024,256]{1,0:T(8,128)} convert(bf16[1024,256]{1,0:T(8,128)(2,1)} %shard_map.109) | non-fusion elementwise | flops 262144 | bytes 1572864 | tf_op jit(solution)/shard_map/convert_element_type | solution.py:209
  (52 shorter events, 5.6 us)
Async XLA Ops:
  2.5 7.5 %copy-start.2 = (bf16[512,512]{1,0:T(8,128)(2,1)S(1)}, bf16[512,512]{1,0:T(8,128)(2,1)}, u32[]{:S(2)}) copy-start(bf16[512,512]{1,0:T(8,128)(2,1)} %constant.58.clone) | copy-start | bytes 1572868
  10.4 1.1 %copy-start.6 = (s32[2,256]{1,0:T(2,128)S(1)}, s32[2,256]{1,0:T(2,128)}, u32[]{:S(2)}) copy-start(s32[2,256]{1,0:T(2,128)} %param.41) | copy-start | bytes 6148
  10.4 1.1 %copy-start.7 = (s32[2,256]{1,0:T(2,128)S(1)}, s32[2,256]{1,0:T(2,128)}, u32[]{:S(2)}) copy-start(s32[2,256]{1,0:T(2,128)} %param.42) | copy-start | bytes 6148
  12.0 60.0 %collective-permute-start.42 = (bf16[1040,256]{1,0:T(8,128)(2,1)S(1)}, bf16[1040,256]{1,0:T(8,128)(2,1)S(1)}, u32[]{:S(2)}, u32[]{:S(2)}) collective-permute-start(bf16[1040,256]{1,0:T(8,128)(2,1)S(1)} %copy.49), channel_id=1, source_target_pairs={{0,30},{2,28},{4,26},{6,24},{8,22},{10,20},{12,18},{14,16},{16,14}... | collective-permute-start | bytes 1597448 | tf_op jit(solution)/shard_map/ppermute | solution.py:57
  23.1 43.6 %collective-permute-start.11 = (bf16[1040,256]{1,0:T(8,128)(2,1)S(1)}, bf16[1040,256]{1,0:T(8,128)(2,1)}, u32[]{:S(2)}, u32[]{:S(2)}) collective-permute-start(bf16[1040,256]{1,0:T(8,128)(2,1)S(1)} %copy.61), channel_id=1, source_target_pairs={{0,24},{2,26},{4,28},{6,30},{8,16},{10,18},{12,20},{14,22},{16,8},... | collective-permute-start | bytes 1597448 | tf_op jit(solution)/shard_map/cond/branch_11_fun/ppermute | solution.py:57
  67.4 2.1 %copy-start.1 = (bf16[512,512]{1,0:T(8,128)(2,1)S(1)}, bf16[512,512]{1,0:T(8,128)(2,1)}, u32[]{:S(2)}) copy-start(bf16[512,512]{1,0:T(8,128)(2,1)} %constant.63) | copy-start | bytes 1572868
  69.6 1.0 copy-start
  69.6 1.0 copy-start.4
  70.6 1.0 copy-start.3
  70.6 1.0 copy-start.5
  71.4 3.6 %collective-permute-start.44 = (bf16[512,256]{1,0:T(8,128)(2,1)S(1)}, bf16[512,256]{1,0:T(8,128)(2,1)S(1)}, u32[]{:S(2)}, u32[]{:S(2)}) collective-permute-start(bf16[512,256]{1,0:T(8,128)(2,1)S(1)} %select_convert_fusion), channel_id=1, source_target_pairs={{0,1},{1,0},{2,3},{3,2},{4,5},{5,4},{6,7},{7,6},{8,9},{9,8},{10,11... | collective-permute-start | bytes 786440 | tf_op jit(solution)/shard_map/ppermute | solution.py:191
  74.6 1.6 %collective-permute-start.43 = (bf16[512,256]{1,0:T(8,128)(2,1)S(1)}, bf16[512,256]{1,0:T(8,128)(2,1)S(1)}, u32[]{:S(2)}, u32[]{:S(2)}) collective-permute-start(bf16[512,256]{1,0:T(8,128)(2,1)S(1)} %select_convert_fusion.1), channel_id=1, source_target_pairs={{0,1},{1,0},{2,3},{3,2},{4,5},{5,4},{6,7},{7,6},{8,9},{9,8},{10,11... | collective-permute-start | bytes 786440 | tf_op jit(solution)/shard_map/ppermute | solution.py:191
  76.4 8.3 %collective-permute-start.36 = (bf16[256,256]{1,0:T(8,128)(2,1)S(1)}, bf16[256,256]{1,0:T(8,128)(2,1)}, u32[]{:S(2)}, u32[]{:S(2)}) collective-permute-start(bf16[256,256]{1,0:T(8,128)(2,1)S(1)} %slice.166), channel_id=1, source_target_pairs={{0,30},{2,28},{4,26},{6,24},{8,22},{10,20},{12,18},{14,16},{16,14}... | collective-permute-start | bytes 393224 | tf_op jit(solution)/shard_map/cond/branch_11_fun/ppermute | solution.py:57
  79.0 7.1 %collective-permute-start.37 = (bf16[256,256]{1,0:T(8,128)(2,1)S(1)}, bf16[256,256]{1,0:T(8,128)(2,1)}, u32[]{:S(2)}, u32[]{:S(2)}) collective-permute-start(bf16[256,256]{1,0:T(8,128)(2,1)S(1)} %slice.180), channel_id=1, source_target_pairs={{0,24},{2,26},{4,28},{6,30},{8,16},{10,18},{12,20},{14,22},{16,8},... | collective-permute-start | bytes 393224 | tf_op jit(solution)/shard_map/cond/branch_11_fun/ppermute | solution.py:57
